TPU v7x, 512 devices: a whole 4x4x16 slice. The times are simulated.
512 devices in a mesh: span: 32 (over z_lo, x), stream: 16 (over z_hi, y, core).
Axes of the slice: x: 4, y: 4, z: 16 (z_hi: 2, z_lo: 8; z = z_hi * 8 + z_lo), core: 2. Of those that a mesh axis runs over, the one named last changes fastest.
Arguments:
- divergence: bfloat16 [1536, 512, 256], P('span', 'stream'), may hold values from -6 to 6
- flow_basis: float32 [512, 512], P('stream'), may hold values from -1 to 2
- wall_basis: float32 [256, 256], replicated, may hold values from -1 to 2
- flow_mass: float32 [512], replicated, may hold values from 0.5 to 2
- wall_mass: float32 [256], replicated, may hold values from 0.5 to 2
- flow_eigen: float32 [512], replicated, may hold values from 0.2 to 2
- wall_eigen: float32 [256], replicated, may hold values from 0.2 to 2
Outputs:
- pressure: float32 [1536, 512, 256], P(('span', 'stream'))
All inputs are finite; a program needn't handle non-finite values.
Results may differ from a plain program's by a relative error of at most 0.0023.
Values may be sent and summed in bfloat16 or wider, within the bound.
A program may use at most 64 MiB of HBM per device.

v0:
```python
import math

import jax
import jax.numpy as jnp
from jax import lax
from jax.sharding import PartitionSpec as P


def fourier_rows(field_ids, length):
    midpoint = length // 2
    wavenum = jnp.where(field_ids <= midpoint, field_ids, field_ids - midpoint)
    planes = jnp.arange(length, dtype=jnp.int32)
    phase = wavenum[:, None] * planes[None, :] % length
    angle = phase.astype(jnp.float32) * jnp.float32(2.0 * math.pi / length)
    values = jnp.where((field_ids <= midpoint)[:, None], jnp.cos(angle), -jnp.sin(angle))
    return values.astype(jnp.bfloat16)


def wave_terms(field_ids, length):
    midpoint = length // 2
    wavenum = jnp.where(field_ids <= midpoint, field_ids, field_ids - midpoint).astype(jnp.float32)
    ratio = wavenum / jnp.float32(midpoint)
    return ratio * ratio


def local(divergence, flow_basis, wall_basis, flow_mass, wall_mass, flow_eigen, wall_eigen):
    highest = lax.Precision.HIGHEST
    span_count = lax.axis_size("span")
    flow_count = lax.axis_size("stream")
    plane_count, row_count, wall_count = divergence.shape
    field_count = plane_count * span_count
    owned_fields = plane_count // flow_count
    line_length = row_count * flow_count
    rows_order = jnp.arange(field_count, dtype=jnp.int32)
    table = fourier_rows(rows_order, field_count)
    slab_in = lax.all_to_all(divergence, "span", split_axis=1, concat_axis=0, tiled=True)
    flat = jnp.dot(table, slab_in.reshape(field_count, -1), preferred_element_type=jnp.float32)
    spectral = (flat * float(field_count) ** (-0.5)).reshape(
        field_count, slab_in.shape[1], slab_in.shape[2]
    )
    grouped = lax.all_to_all(spectral, "span", split_axis=0, concat_axis=1, tiled=True)
    lines = lax.all_to_all(grouped, "stream", split_axis=0, concat_axis=1, tiled=True)
    along_wall = jnp.dot(
        (lines * wall_mass[None, None, :]).reshape(-1, wall_count), wall_basis, precision=highest
    )
    weighted = along_wall.reshape(owned_fields, line_length, wall_count) * flow_mass[None, :, None]
    owned_ids = (
        lax.axis_index("span") * plane_count
        + lax.axis_index("stream") * owned_fields
        + jnp.arange(owned_fields, dtype=jnp.int32)
    )
    waves = wave_terms(owned_ids, field_count)
    denominator = flow_eigen[None, :, None] + wall_eigen[None, None, :] + waves[:, None, None]
    coeff = jnp.einsum(
        "xn,fxm->fnm",
        lax.all_gather(flow_basis, "stream", axis=0, tiled=True),
        weighted,
        precision=highest,
    )
    solved = coeff / denominator
    back = jnp.einsum(
        "xn,fnm->fxm",
        lax.all_gather(flow_basis, "stream", axis=0, tiled=True),
        solved,
        precision=highest,
    )
    pressure = jnp.dot(back.reshape(-1, wall_count), wall_basis.T, precision=highest)
    return pressure.reshape(owned_fields, line_length, wall_count)


def solution(mesh):
    return jax.shard_map(
        local,
        mesh=mesh,
        in_specs=(P("span", "stream", None), P("stream", None), P(), P(), P(), P(), P()),
        out_specs=P(("span", "stream"), None, None),
        check_vma=False,
    )
```

profile of v0, /device:TPU:1, one launch (start us, length us, event | category | flops | bytes accessed | tf_op | source)
XLA Modules:
  0.0 348.4 jit_solution(8871368069057873704)
XLA Ops:
  6.5 0.0 copy-start
  6.5 2.5 copy.22
  9.0 15.9 %all-to-all-start = ((bf16[48,32,256]{2,0,1:T(8,128)(2,1)}), bf16[48,32,256]{2,0,1:T(8,128)(2,1)S(1)}, u32[]{:S(2)}, u32[]{:S(2)}) async-start(bf16[48,32,256]{2,0,1:T(8,128)(2,1)} %copy.22), calls=%async_computation | async-start | bytes 1572864 | tf_op jit(solution)/shard_map/all_to_all | solution.py:36
  25.0 37.8 %all-to-all-done = bf16[48,32,256]{2,0,1:T(8,128)(2,1)S(1)} async-done(((bf16[48,32,256]{2,0,1:T(8,128)(2,1)}), bf16[48,32,256]{2,0,1:T(8,128)(2,1)S(1)}, u32[]{:S(2)}, u32[]{:S(2)}) %all-to-all-start) | async-done | bytes 786464 | tf_op jit(solution)/shard_map/all_to_all | solution.py:36
  62.8 52.7 %fusion.8 = f32[1536,1,256]{2,0,1:T(8,128)S(1)} fusion(bf16[1536,256]{1,0:T(8,128)(2,1)S(1)} %bitcast.39, s32[1536]{0:T(1024)S(1)} %add_select_fusion.1, pred[1536]{0:T(1024)(128)(4,1)S(1)} %iota_compare_fusion), kind=kOutput, calls=%fused_computation.11 | convolution fusion | flops 1236664320 | bytes 2366976 | tf_op jit(solution)/shard_map/dot_general | solution.py:37
  115.5 6.5 %copy.23 = f32[1536,1,256]{2,1,0:T(1,128)S(1)} copy(f32[1536,1,256]{2,0,1:T(8,128)S(1)} %fusion.8) | data formatting | bytes 3145728 | tf_op jit(solution)/shard_map/reshape | solution.py:38
  122.0 82.2 %all_to_all.51 = f32[1536,1,256]{2,1,0:T(1,128)S(1)} all-to-all(f32[1536,1,256]{2,1,0:T(1,128)S(1)} %copy.23), channel_id=1, replica_groups=mesh['span'=32,'stream'=16] {'span'}, dimensions={0} | all-to-all | bytes 3145728 | tf_op jit(solution)/shard_map/all_to_all | solution.py:41
  204.2 0.1 copy.30
  204.3 2.1 copy.24
  206.4 0.0 copy-start.2
  206.4 0.0 copy-start.4
  206.4 12.7 %all-to-all-start.2 = ((f32[48,32,256]{2,1,0:T(8,128)}), f32[48,32,256]{2,1,0:T(8,128)S(1)}, u32[]{:S(2)}, u32[]{:S(2)}) async-start(f32[48,32,256]{2,1,0:T(8,128)} %copy.24), calls=%async_computation.2 | async-start | bytes 3145728 | tf_op jit(solution)/shard_map/all_to_all | solution.py:42
  219.0 0.2 all-gather.2.cloned.1.call-start
  219.3 0.5 all-gather.2.cloned.1.call-update
  219.8 0.0 copy-done.2
  219.8 0.0 copy-done.4
  219.8 0.1 broadcast_add_fusion
  219.9 56.0 %all-to-all-done.2 = f32[48,32,256]{2,1,0:T(8,128)S(1)} async-done(((f32[48,32,256]{2,1,0:T(8,128)}), f32[48,32,256]{2,1,0:T(8,128)S(1)}, u32[]{:S(2)}, u32[]{:S(2)}) %all-to-all-start.2) | async-done | bytes 1572896 | tf_op jit(solution)/shard_map/all_to_all | solution.py:42
  275.9 0.0 copy-start.5
  275.9 0.2 copy.25
  276.1 0.5 copy-done.5
  276.6 0.1 bitcast_multiply_fusion
  276.8 0.0 copy-done
  276.8 0.0 copy-start.3
  276.8 1.4 fusion.21
  278.2 52.6 %all-gather.2.cloned.1.call-done = f32[512,512]{1,0:T(8,128)} async-done(((f32[32,512]{1,0:T(8,128)}), f32[512,512]{1,0:T(8,128)}) %all-gather.2.cloned.1.call-update) | async-done | bytes 1048592 | tf_op jit(solution)/shard_map/all_gather | solution.py:56
  330.8 0.0 copy-done.3
  330.8 0.0 copy-start.1
  330.8 4.1 %fusion.13 = f32[3,256,512]{2,1,0:T(8,128)S(1)} fusion(f32[3,512,256]{2,1,0:T(8,128)S(1)} %fusion.21, f32[512,512]{1,0:T(8,128)} %all-gather.2.cloned.1.call-done, f32[512]{0:T(512)S(1)} %copy-done.3), kind=kOutput, calls=%fused_computation.18 | convolution fusion | flops 2416312320 | bytes 4196352 | tf_op jit(solution)/shard_map/xn,fxm->fnm/dot_general | solution.py:54
  334.9 0.0 copy-done.1
  334.9 2.8 fusion.11
  337.7 3.9 %fusion.9 = f32[3,512,256]{2,1,0:T(8,128)} fusion(f32[3,256,512]{2,1,0:T(8,128)S(1)} %fusion.11, f32[256,256]{1,0:T(8,128)S(1)} %copy-done), kind=kOutput, calls=%fused_computation.12 | convolution fusion | flops 1207959552 | bytes 3407872 | tf_op jit(solution)/shard_map/dot_general | solution.py:67
  (3 shorter events, 0.0 us)
Async XLA Ops:
  6.5 270.2 %copy-start = (f32[256,256]{1,0:T(8,128)S(1)}, f32[256,256]{1,0:T(8,128)}, u32[]{:S(2)}) copy-start(f32[256,256]{1,0:T(8,128)} %param.9) | copy-start | bytes 786436
  9.0 53.7 %all-to-all-start = ((bf16[48,32,256]{2,0,1:T(8,128)(2,1)}), bf16[48,32,256]{2,0,1:T(8,128)(2,1)S(1)}, u32[]{:S(2)}, u32[]{:S(2)}) async-start(bf16[48,32,256]{2,0,1:T(8,128)(2,1)} %copy.22), calls=%async_computation | async-start | bytes 1572864 | tf_op jit(solution)/shard_map/all_to_all | solution.py:36
  206.4 13.4 %copy-start.2 = (f32[512]{0:T(512)S(1)}, f32[512]{0:T(512)}, u32[]{:S(2)}) copy-start(f32[512]{0:T(512)} %param.12) | copy-start | bytes 6148
  206.4 13.4 %copy-start.4 = (f32[256]{0:T(256)S(1)}, f32[256]{0:T(256)}, u32[]{:S(2)}) copy-start(f32[256]{0:T(256)} %param.13) | copy-start | bytes 3076
  206.4 69.6 %all-to-all-start.2 = ((f32[48,32,256]{2,1,0:T(8,128)}), f32[48,32,256]{2,1,0:T(8,128)S(1)}, u32[]{:S(2)}, u32[]{:S(2)}) async-start(f32[48,32,256]{2,1,0:T(8,128)} %copy.24), calls=%async_computation.2 | async-start | bytes 3145728 | tf_op jit(solution)/shard_map/all_to_all | solution.py:42
  219.0 111.8 %all-gather.2.cloned.1.call-start = ((), (), s32[]{:S(2)}) async-start(), calls=%async_computation.3 | async-start | bytes 1114112 | tf_op jit(solution)/shard_map/all_gather | solution.py:56
  275.9 0.7 copy-start.5
  276.8 54.0 %copy-start.3 = (f32[512]{0:T(512)S(1)}, f32[512]{0:T(512)}, u32[]{:S(2)}) copy-start(f32[512]{0:T(512)} %param.10) | copy-start | bytes 6148
  330.8 4.1 %copy-start.1 = (f32[512,512]{1,0:T(8,128)S(1)}, f32[512,512]{1,0:T(8,128)}, u32[]{:S(2)}) copy-start(f32[512,512]{1,0:T(8,128)} %all-gather.2.cloned.1.call-done) | copy-start | bytes 3145732
Sparse Core Ops, SparseCore 0:
  223.2 107.5 all-gather.1
where the time goes:
time: 349 us; the launch traced here: 348 us
  waiting for transfers between devices  147 us (42%)
  blocking collectives  82.2 us (24%)
  matrix products  64.8 us (19%)
  starting transfers between devices  28.8 us (8%)
  between operations  13.5 us (4%)
  local copies, waits for them, and re-layouts  11.8 us (3%)
    all_to_all x1, blocking collectives, local(): lax.all_to_all(spectral, 'span', split_axis=0, concat_axis=1, tiled=True)  82.2 us
    all_to_all x1, waiting for transfers between devices, local(): lax.all_to_all(grouped, 'stream', split_axis=0, concat_axis=1, tiled=True)  56 us
    dot_general x1, matrix products, local(): jnp.dot(table, slab_in.reshape(field_count, -1), preferred_element_type=j...  52.7 us
    all_gather x1, waiting for transfers between devices, local(): lax.all_gather(flow_basis, 'stream', axis=0, tiled=True)  52.6 us
    all_to_all x1, waiting for transfers between devices, local(): lax.all_to_all(divergence, 'span', split_axis=1, concat_axis=0, tiled=True)  37.8 us
    all_to_all x1, starting transfers between devices, local(): lax.all_to_all(divergence, 'span', split_axis=1, concat_axis=0, tiled=True)  15.9 us
    all_to_all x1, starting transfers between devices, local(): lax.all_to_all(grouped, 'stream', split_axis=0, concat_axis=1, tiled=True)  12.7 us
  transfers between devices with their start and end apart: 3, of which 3 were waited for; matrix products, arithmetic and copies ran while one was open for 1% of the time, Pallas kernels for 0%

commit v1 on v0

v1 whole, which is shorter than its diff:
```python
import functools
import math

import jax
import jax.numpy as jnp
import numpy as np
from jax import lax
from jax.experimental import pallas as pl
from jax.experimental.pallas import tpu as pltpu
from jax.sharding import PartitionSpec as P

NZ, NX, NY = 1536, 512, 256
MESH = pl.DeviceIdType.MESH
CHUNKS = 4
BF, F32 = jnp.bfloat16, jnp.float32


def table_sets():
    planes = np.arange(NZ)
    sets = []
    for g in range(2):
        fields = []
        for d in range(16):
            fields += [48 * d + 24 * g + r for r in range(24)]
            fields += [48 * (16 + d) + 24 * (1 - g) + r for r in range(24)]
        f = np.array(fields)
        k = np.where(f <= NZ // 2, f, f - NZ // 2)
        angle = ((k[:, None] * planes[None, :]) % NZ).astype(np.float32) * np.float32(2.0 * math.pi / NZ)
        sets.append(np.where((f <= NZ // 2)[:, None], np.cos(angle), -np.sin(angle)))
    return np.stack(sets).astype(jnp.bfloat16)


def split(a):
    hi = a.astype(BF)
    return hi, (a - hi.astype(F32)).astype(BF)


def dot(a, b):
    return jnp.dot(a, b, preferred_element_type=F32)


def forward_kernel(
    div, flow, table, fmass, wall, wmass,
    proj, fhi, flo, whi, wlo, thi, tlo,
    tbl, slab, spec, abuf, bbuf, lines, perm, gath, fmthi, fmtlo,
    tsem, rsem1, rsema, rsemb, ssem1, ssema, ssemb, gsem, gssem,
):
    s, t = lax.axis_index("span"), lax.axis_index("stream")
    h, d = s // 16, s % 16
    zh, u = t // 8, t % 8
    g = lax.rem(h + zh, 2)

    def span_peer(k):
        other = k // 16
        return lax.rem(h + 1 + other, 2) * 16 + lax.rem(d + k, 16)

    def stream_peer(k):
        own = k // 8
        sp = lax.rem(h + 1 + own, 2) * 16 + d
        tp = lax.rem(zh + 1 + own, 2) * 8 + lax.rem(u + k, 8)
        return sp, tp

    tcopy = pltpu.make_async_copy(table.at[g], tbl, tsem)
    tcopy.start()

    barrier = pltpu.get_barrier_semaphore()

    def greet_span(k, _):
        pl.semaphore_signal(barrier, inc=1, device_id=(span_peer(k), t), device_id_type=MESH)
        return 0

    def greet_stream(k, _):
        pl.semaphore_signal(barrier, inc=1, device_id=stream_peer(k), device_id_type=MESH)
        return 0

    lax.fori_loop(0, 16, greet_span, 0)
    lax.fori_loop(17, 32, greet_span, 0)
    lax.fori_loop(0, 8, greet_stream, 0)
    lax.fori_loop(9, 16, greet_stream, 0)
    pl.semaphore_wait(barrier, 46)

    own_rows = gath.at[pl.ds(pl.multiple_of(t * 32, 32), 32), :]
    pltpu.make_async_copy(flow, own_rows, gsem.at[0]).start()
    pltpu.make_async_remote_copy(
        src_ref=flow, dst_ref=own_rows, send_sem=gssem, recv_sem=gsem.at[1],
        device_id=((1 - h) * 16 + d, (1 - zh) * 8 + u), device_id_type=MESH,
    ).start()

    def share_flow(k, _):
        pltpu.make_async_remote_copy(
            src_ref=flow, dst_ref=own_rows, send_sem=gssem, recv_sem=gsem.at[0],
            device_id=stream_peer(k), device_id_type=MESH,
        ).start()
        return 0

    lax.fori_loop(9, 16, share_flow, 0)

    def send1(c):
        rows = slab.at[c, pl.ds(pl.multiple_of(s * 48, 48), 48), :]

        def one(k, _):
            dst = span_peer(k)
            pltpu.make_async_remote_copy(
                src_ref=div.at[lax.rem(dst, 16), c], dst_ref=rows, send_sem=ssem1.at[c], recv_sem=rsem1.at[c],
                device_id=(dst, t), device_id_type=MESH,
            ).start()
            return 0

        pltpu.make_async_copy(div.at[d, c], rows, rsem1.at[c]).start()
        lax.fori_loop(0, 16, one, 0)
        lax.fori_loop(17, 32, one, 0)

    def wait1(c):
        pltpu.make_async_copy(slab.at[c], slab.at[c], rsem1.at[c]).wait()

    def transform(c):
        def tile(i, _):
            rows = pl.ds(pl.multiple_of(i * 256, 256), 256)
            r = dot(tbl[rows, :], slab[c]) * F32(float(NZ) ** -0.5)
            spec[c, rows, :] = r.astype(BF)
            return 0

        lax.fori_loop(0, 3, tile, 0)

    def senda(c):
        def one(k, _):
            dd = lax.rem(d + k, 16)
            pltpu.make_async_remote_copy(
                src_ref=spec.at[c, pl.ds(pl.multiple_of(dd * 48, 48), 48), :], dst_ref=abuf.at[c, d],
                send_sem=ssema.at[c], recv_sem=rsema.at[c],
                device_id=(h * 16 + dd, t), device_id_type=MESH,
            ).start()
            return 0

        pltpu.make_async_copy(spec.at[c, pl.ds(pl.multiple_of(d * 48, 48), 48), :], abuf.at[c, d], rsema.at[c]).start()
        lax.fori_loop(1, 16, one, 0)

    def waita(c):
        pltpu.make_async_copy(abuf.at[c], abuf.at[c], rsema.at[c]).wait()

    def turn(c):
        def tile(i, _):
            rows = pl.ds(pl.multiple_of(i * 256, 256), 256)
            r = dot(perm[rows, :], abuf[c].reshape(768, 128))
            bbuf[c, pl.ds(pl.multiple_of(i * 16, 16), 16)] = r.reshape(16, 16, 128).astype(BF)
            return 0

        lax.fori_loop(0, 3, tile, 0)

    def sendb(c):
        dst_ref = lines.at[c, :, pl.ds(pl.multiple_of(t * 16, 16), 16), :]

        def one(k, _):
            sp, tp = stream_peer(k)
            pltpu.make_async_remote_copy(
                src_ref=bbuf.at[c, pl.ds((sp // 16) * 24 + lax.rem(tp, 8) * 3, 3)], dst_ref=dst_ref,
                send_sem=ssemb.at[c], recv_sem=rsemb.at[c],
                device_id=(sp, tp), device_id_type=MESH,
            ).start()
            return 0

        lax.fori_loop(0, 8, one, 0)
        pltpu.make_async_copy(bbuf.at[c, pl.ds(h * 24 + u * 3, 3)], dst_ref, rsemb.at[c]).start()
        lax.fori_loop(9, 16, one, 0)

    def waitb(c):
        pltpu.make_async_copy(lines.at[c], lines.at[c], rsemb.at[c]).wait()

    def project(c):
        xp, yh = c // 2, c % 2

        def field(f, _):
            part = dot(fmthi[xp], lines[c, f]) + dot(fmtlo[xp], lines[c, f])
            cols = pl.ds(yh * 128, 128)
            if xp == 0:
                proj[f, :, cols] = part
            else:
                proj[f, :, cols] += part
            return 0

        lax.fori_loop(0, 3, field, 0)

    send1(0)
    send1(1)

    i0 = lax.broadcasted_iota(jnp.int32, (768, 768), 0)
    i1 = lax.broadcasted_iota(jnp.int32, (768, 768), 1)
    perm[...] = jnp.where(lax.rem(i0, 16) * 48 + i0 // 16 == i1, 1.0, 0.0).astype(BF)

    w = wall[...]
    thi[...], tlo[...] = split(w.T)
    wm = jnp.broadcast_to(wmass[...], (128, NY)).T
    for j in range(NY // 128):
        cols = slice(j * 128, (j + 1) * 128)
        whi[:, cols], wlo[:, cols] = split(w[:, cols] * wm)

    far = (1 - zh) * 8 + u
    far_rows = gath.at[pl.ds(pl.multiple_of(far * 32, 32), 32), :]
    pltpu.make_async_copy(far_rows, far_rows, gsem.at[1]).wait()

    def pass_on(k, _):
        pltpu.make_async_remote_copy(
            src_ref=far_rows, dst_ref=far_rows, send_sem=gssem, recv_sem=gsem.at[2],
            device_id=stream_peer(k), device_id_type=MESH,
        ).start()
        return 0

    lax.fori_loop(9, 16, pass_on, 0)
    near = gath.at[pl.ds(0, 256), :]
    pltpu.make_async_copy(near, near, gsem.at[0]).wait()
    rest = gath.at[pl.ds(0, 224), :]
    pltpu.make_async_copy(rest, rest, gsem.at[2]).wait()

    fhi[...], flo[...] = split(gath[...])
    fm = jnp.broadcast_to(fmass[...], (128, NX)).T
    for j in range(NX // 128):
        cols = slice(j * 128, (j + 1) * 128)
        scaled = (gath[:, cols] * fm).reshape(16, 2, 16, 128)
        for xp in range(2):
            fmthi[xp, cols, :], fmtlo[xp, cols, :] = split(scaled[:, xp].reshape(256, 128).T)

    tcopy.wait()
    for c in range(CHUNKS + 2):
        if c < CHUNKS:
            wait1(c)
            transform(c)
            senda(c)
            if c + 2 < CHUNKS:
                send1(c + 2)
        if 1 <= c <= CHUNKS:
            waita(c - 1)
            turn(c - 1)
            sendb(c - 1)
        if c >= 2:
            waitb(c - 2)
            project(c - 2)

    sent = gath.at[pl.ds(0, 480), :]
    pltpu.make_async_copy(sent, sent, gssem).wait()
    for c in range(CHUNKS):
        r1 = slab.at[c, pl.ds(0, 31 * 48), :]
        pltpu.make_async_copy(r1, r1, ssem1.at[c]).wait()
        ra = spec.at[c, pl.ds(0, 15 * 48), :]
        pltpu.make_async_copy(ra, ra, ssema.at[c]).wait()
        rb = bbuf.at[c, pl.ds(0, 45)]
        pltpu.make_async_copy(rb, rb, ssemb.at[c]).wait()


def solve_kernel(proj, fhi, flo, whi, wlo, thi, tlo, feig, weig, out):
    s, t = lax.axis_index("span"), lax.axis_index("stream")
    f = s * 48 + t * 3 + pl.program_id(0)
    k = jnp.where(f <= NZ // 2, f, f - NZ // 2).astype(F32) / F32(NZ // 2)
    ahi, alo = split(proj[0])
    coeff = dot(ahi, whi[...]) + (dot(ahi, wlo[...]) + dot(alo, whi[...]))
    fe = jnp.broadcast_to(feig[...], (128, NX)).T
    denom = jnp.concatenate([fe, fe], axis=1) + weig[...] + k * k
    shi, slo = split(coeff / denom)
    back = dot(fhi[...], shi) + (dot(fhi[...], slo) + dot(flo[...], shi))
    bhi, blo = split(back)
    out[0] = dot(bhi, thi[...]) + (dot(bhi, tlo[...]) + dot(blo, thi[...]))


def local(divergence, flow_basis, wall_basis, flow_mass, wall_mass, flow_eigen, wall_eigen):
    blocks = divergence.reshape(48, 2, 16, 2, 128).transpose(2, 1, 3, 0, 4).reshape(16, CHUNKS, 48, 128)
    table = jnp.asarray(table_sets())
    vmem = pl.BlockSpec(memory_space=pltpu.VMEM)
    hbm = pl.BlockSpec(memory_space=pl.ANY)
    sds = jax.ShapeDtypeStruct
    proj, fhi, flo, whi, wlo, thi, tlo = pl.pallas_call(
        forward_kernel,
        out_shape=[
            sds((3, NX, NY), F32), sds((NX, NX), BF), sds((NX, NX), BF),
            sds((NY, NY), BF), sds((NY, NY), BF), sds((NY, NY), BF), sds((NY, NY), BF),
        ],
        in_specs=[hbm, vmem, hbm, vmem, vmem, vmem],
        out_specs=[vmem] * 7,
        scratch_shapes=[
            pltpu.VMEM((768, NZ), BF),
            pltpu.VMEM((CHUNKS, NZ, 128), BF),
            pltpu.VMEM((CHUNKS, 768, 128), BF),
            pltpu.VMEM((CHUNKS, 16, 48, 128), BF),
            pltpu.VMEM((CHUNKS, 48, 16, 128), BF),
            pltpu.VMEM((CHUNKS, 3, 256, 128), BF),
            pltpu.VMEM((768, 768), BF),
            pltpu.VMEM((NX, NX), F32),
            pltpu.VMEM((2, NX, 256), BF),
            pltpu.VMEM((2, NX, 256), BF),
            pltpu.SemaphoreType.DMA,
            pltpu.SemaphoreType.DMA((CHUNKS,)),
            pltpu.SemaphoreType.DMA((CHUNKS,)),
            pltpu.SemaphoreType.DMA((CHUNKS,)),
            pltpu.SemaphoreType.DMA((CHUNKS,)),
            pltpu.SemaphoreType.DMA((CHUNKS,)),
            pltpu.SemaphoreType.DMA((CHUNKS,)),
            pltpu.SemaphoreType.DMA((3,)),
            pltpu.SemaphoreType.DMA,
        ],
        compiler_params=pltpu.CompilerParams(collective_id=0, has_side_effects=True, vmem_limit_bytes=40 << 20),
    )(blocks, flow_basis, table, flow_mass.reshape(1, NX), wall_basis, wall_mass.reshape(1, NY))

    whole = lambda a: pl.BlockSpec(a.shape, lambda f: (0, 0))
    row_feig, row_weig = flow_eigen.reshape(1, NX), wall_eigen.reshape(1, NY)
    fixed = [fhi, flo, whi, wlo, thi, tlo, row_feig, row_weig]
    plane = pl.BlockSpec((1, NX, NY), lambda f: (f, 0, 0))
    return pl.pallas_call(
        solve_kernel,
        out_shape=sds((3, NX, NY), F32),
        grid=(3,),
        in_specs=[plane] + [whole(a) for a in fixed],
        out_specs=plane,
        compiler_params=pltpu.CompilerParams(vmem_limit_bytes=40 << 20),
    )(proj, *fixed)


def solution(mesh):
    return jax.shard_map(
        local,
        mesh=mesh,
        in_specs=(P("span", "stream", None), P("stream", None), P(), P(), P(), P(), P()),
        out_specs=P(("span", "stream"), None, None),
        check_vma=False,
    )
```

time: 349 us -> 129 us (0.37)
  waiting for transfers between devices: 147 us -> 0 us
  Pallas kernels: 0 us -> 123 us
  blocking collectives: 82.2 us -> 0 us
  matrix products: 64.8 us -> 0 us
  starting transfers between devices: 28.8 us -> 0 us
  between operations: 13.5 us -> 0.09 us
  local copies, waits for them, and re-layouts: 11.8 us -> 5.33 us
    pallas_call x0 -> x2, Pallas kernels: none -> 123 us  [the longest x1 117 us: local(): pl.pallas_call(forward_kernel, out_shape=[sds((3, NX, NY), F32), sds((NX,...]
    all_to_all x2 -> x0, waiting for transfers between devices: 93.8 us -> none  [the longest x1 56 us: local(): lax.all_to_all(grouped, 'stream', split_axis=0, concat_axis=1, tiled=True)]
    all_to_all x1 -> x0, blocking collectives: 82.2 us -> none  [local(): lax.all_to_all(spectral, 'span', split_axis=0, concat_axis=1, tiled=True)]
    dot_general x5 -> x0, matrix products: 64.8 us -> none  [the longest x1 52.7 us: local(): jnp.dot(table, slab_in.reshape(field_count, -1), preferred_element_type=j...]
    all_gather x1 -> x0, waiting for transfers between devices: 52.6 us -> none  [local(): lax.all_gather(flow_basis, 'stream', axis=0, tiled=True)]
    all_to_all x2 -> x0, starting transfers between devices: 28.6 us -> none  [the longest x1 15.9 us: local(): lax.all_to_all(divergence, 'span', split_axis=1, concat_axis=0, tiled=True)]
  transfers between devices with their start and end apart: 3 -> 0, of which waited for: 3 -> 0; matrix products, arithmetic and copies ran while one was open for 1% -> 0% of each run, Pallas kernels for 0% -> 0%
where the time goes in v1:
time: 129 us; the launch traced here: 128 us
  Pallas kernels  123 us (95%)
  local copies, waits for them, and re-layouts  5.33 us (4%)
    pallas_call x1, Pallas kernels, local(): pl.pallas_call(forward_kernel, out_shape=[sds((3, NX, NY), F32), sds((NX,...  117 us
    pallas_call x1, Pallas kernels, local(): pl.pallas_call(solve_kernel, out_shape=sds((3, NX, NY), F32), grid=(3,),...  6.26 us
    reshape x2, local copies, waits for them, and re-layouts, local(): divergence.reshape(48, 2, 16, 2, 128).transpose(2, 1, 3, 0, 4)  2.98 us

profile of v1, /device:TPU:1, one launch (start us, length us, event | category | flops | bytes accessed | tf_op | source)
XLA Modules:
  0.0 128.4 jit_solution(15058868721934778171)
XLA Ops:
  0.0 0.0 copy-start.1
  0.0 0.0 copy-start.2
  0.0 0.0 copy-start.3
  0.0 0.0 copy-start.5
  0.0 2.1 %reshape.18 = bf16[48,2,16,2,128]{4,3,2,1,0:T(2,128)(2,1)S(1)} reshape(bf16[48,32,256]{2,1,0:T(8,128)(2,1)} %param.8) | data formatting | bytes 1572864 | tf_op jit(solution)/shard_map/reshape | solution.py:264
  2.1 0.9 copy.9
  3.0 0.0 copy-done.1
  3.0 0.0 copy-done.2
  3.0 0.0 copy-done.3
  3.0 0.0 copy-done.5
  3.1 0.0 copy-start
  3.1 2.3 %copy-done = bf16[2,768,1536]{2,1,0:T(8,128)(2,1)S(1)} copy-done((bf16[2,768,1536]{2,1,0:T(8,128)(2,1)S(1)}, bf16[2,768,1536]{2,1,0:T(8,128)(2,1)}, u32[]{:S(2)}) %copy-start) | copy-done | bytes 4718616
  5.4 0.0 copy-start.4
  5.4 0.0 copy-start.6
  5.4 116.7 %shard_map.82 = (f32[3,512,256]{2,1,0:T(8,128)S(1)}, bf16[512,512]{1,0:T(8,128)(2,1)S(1)}, bf16[512,512]{1,0:T(8,128)(2,1)S(1)}, bf16[256,256]{1,0:T(8,128)(2,1)...) custom-call(bf16[16,4,48,128]{3,2,1,0:T(8,128)(2,1)S(1)} %bitcast.7, ...), custom_call_target="tpu_custom_call" | custom-call | tf_op jit(solution)/shard_map/pallas_call | solution.py:269
  122.1 0.0 copy-done.4
  122.1 0.0 copy-done.6
  122.1 6.3 %shard_map.83 = f32[3,512,256]{2,1,0:T(8,128)} custom-call(f32[3,512,256]{2,1,0:T(8,128)S(1)} %get-tuple-element.12.proj, bf16[512,512]{1,0:T(8,128)(2,1)S(1)} %get-tuple-element.13.fhi, bf16[512,512]{1,0:T(8,128)(2,1)S(1)} %get-tuple-element.14.flo, bf16[256,256]{1,0:T(8,128)(2,1)S(1)} %get-tuple-element.15.whi, ...), custom_call_target="tpu_custom_call" | custom-call | tf_op jit(solution)/shard_map/pallas_call | solution.py:305
Async XLA Ops:
  0.0 3.0 %copy-start.1 = (f32[256,256]{1,0:T(8,128)S(1)}, f32[256,256]{1,0:T(8,128)}, u32[]{:S(2)}) copy-start(f32[256,256]{1,0:T(8,128)} %wall.1) | copy-start | bytes 786436
  0.0 3.0 %copy-start.2 = (f32[32,512]{1,0:T(8,128)S(1)}, f32[32,512]{1,0:T(8,128)}, u32[]{:S(2)}) copy-start(f32[32,512]{1,0:T(8,128)} %flow.1) | copy-start | bytes 196612
  0.0 3.0 %copy-start.3 = (f32[512]{0:T(512)S(1)}, f32[512]{0:T(512)}, u32[]{:S(2)}) copy-start(f32[512]{0:T(512)} %param.11) | copy-start | bytes 6148
  0.0 3.0 %copy-start.5 = (f32[256]{0:T(256)S(1)}, f32[256]{0:T(256)}, u32[]{:S(2)}) copy-start(f32[256]{0:T(256)} %param.12) | copy-start | bytes 3076
  3.1 2.3 %copy-start = (bf16[2,768,1536]{2,1,0:T(8,128)(2,1)S(1)}, bf16[2,768,1536]{2,1,0:T(8,128)(2,1)}, u32[]{:S(2)}) copy-start(bf16[2,768,1536]{2,1,0:T(8,128)(2,1)} %constant.2.clone.table) | copy-start | bytes 14155780
  5.4 116.7 %copy-start.4 = (f32[512]{0:T(512)S(1)}, f32[512]{0:T(512)}, u32[]{:S(2)}) copy-start(f32[512]{0:T(512)} %param.13) | copy-start | bytes 6148
  5.4 116.7 %copy-start.6 = (f32[256]{0:T(256)S(1)}, f32[256]{0:T(256)}, u32[]{:S(2)}) copy-start(f32[256]{0:T(256)} %param.14) | copy-start | bytes 3076

commit v2 on v0

v2 whole, which is shorter than its diff:
```python
import math

import jax
import jax.numpy as jnp
from jax import lax
from jax.experimental import pallas as pl
from jax.experimental.pallas import tpu as pltpu
from jax.sharding import PartitionSpec as P

NZ, NX, NY = 1536, 512, 256
MESH = pl.DeviceIdType.MESH
VMEM_LIMIT = 63 << 20
BF, F32 = jnp.bfloat16, jnp.float32


def turn_values(quarters, shift):
    nearest = jnp.floor(quarters + 0.5)
    r = (quarters - nearest) * F32(math.pi / 2)
    n = nearest.astype(jnp.int32) + shift
    q = r * r
    cos = 1.0 + q * (-0.5 + q * (F32(1 / 24) + q * (F32(-1 / 720) + q * F32(1 / 40320))))
    sin = r * (1.0 + q * (F32(-1 / 6) + q * (F32(1 / 120) + q * (F32(-1 / 5040) + q * F32(1 / 362880)))))
    odd = (n & 1) == 1
    c = jnp.where(odd, sin, cos)
    s = jnp.where(odd, cos, sin)
    return jnp.where(((n + 1) & 2) == 2, -c, c), jnp.where((n & 2) == 2, -s, s)


def table_rows(i, part, store):
    row = lax.broadcasted_iota(jnp.int32, (128, 128), 0) + 128 * part
    plane = lax.broadcasted_iota(jnp.int32, (128, 128), 1)
    field = 48 * (row & 31) + 24 * ((row >> 5) & 1) + 3 * (row >> 6) + i
    sine = field > NZ // 2
    wavenum = jnp.where(sine, field - NZ // 2, field)
    shift = jnp.where(sine, 1, 0)

    def values(product, shift):
        phase = product.astype(F32)
        phase = phase - F32(NZ) * jnp.floor(phase * F32(1.0 / NZ))
        return turn_values(phase * F32(4.0 / NZ), shift)

    c, s = values(wavenum * plane, shift)
    step_c, step_s = values(wavenum * 128, jnp.zeros_like(shift))
    for a in range(NZ // 128):
        store(a, c.astype(BF))
        c, s = c * step_c - s * step_s, s * step_c + c * step_s


def split(a):
    hi = a.astype(BF)
    return hi, (a - hi.astype(F32)).astype(BF)


def dot(a, b):
    return jnp.dot(a, b, preferred_element_type=F32)


def poisson_kernel(
    div_in, flow_in, fmass_in, wall_in, wmass_in, feig_in, weig_in,
    out_hbm,
    div, flow, fmass, wall, wmass, feig, weig, out, tbl, sbuf, slab, spec, abuf, bbuf, lines, proj, gath, perm,
    fhi, flo, whi, wlo, thi, tlo, fmthi, fmtlo, denom,
    rsem1, rsema, rsemb, ssem1, ssema, ssemb, gsem, gssem, lsem, osem,
):
    s, t = lax.axis_index("span"), lax.axis_index("stream")
    zl, x = s // 4, s % 4
    zh, u = t // 8, t % 8
    z = zh * 8 + zl

    def loop(first, last, body):
        lax.fori_loop(first, last, lambda k, _: (body(k), 0)[1], 0)

    def remote(src, dst, ssem, rsem, device):
        pltpu.make_async_remote_copy(
            src_ref=src, dst_ref=dst, send_sem=ssem, recv_sem=rsem, device_id=device, device_id_type=MESH
        ).start()

    def wait(ref, sem):
        pltpu.make_async_copy(ref, ref, sem).wait()

    def span_peer(k):
        return lax.rem(s // 16 + 1 + k // 16, 2) * 16 + lax.rem(s + k, 16)

    def ring_peer(k):
        step = k // 4
        hops = jnp.where(step % 2 == 0, 8 - step // 2, 9 + step // 2)
        zz = lax.rem(z + hops, 16)
        return zz // 8, lax.rem(zz, 8) * 4 + lax.rem(x + k, 4)

    def group_peer(k):
        return s, zh * 8 + lax.rem(u + k, 8)

    pltpu.make_async_copy(div_in, div, lsem.at[0]).start()
    pltpu.make_async_copy(flow_in, flow, lsem.at[1]).start()
    small = [(fmass_in, fmass), (wall_in, wall), (wmass_in, wmass), (feig_in, feig), (weig_in, weig)]
    for j, (src, dst) in enumerate(small):
        pltpu.make_async_copy(src, dst, lsem.at[2 + j]).start()

    barrier = pltpu.get_barrier_semaphore()

    def greet(peer):
        pl.semaphore_signal(barrier, inc=1, device_id=peer, device_id_type=MESH)

    def greet_ring(k):
        hh, sp = ring_peer(k)
        greet((sp, hh * 8 + u))

    loop(0, 60, greet_ring)
    loop(61, 64, greet_ring)
    loop(1, 8, lambda k: greet(group_peer(k)))

    i0 = lax.broadcasted_iota(jnp.int32, (256, 256), 0)
    i1 = lax.broadcasted_iota(jnp.int32, (256, 256), 1)
    perm[...] = jnp.where(lax.rem(i0, 16) * 16 + i0 // 16 == i1, 1.0, 0.0).astype(BF)

    def gather_nodes(j):
        xp, rows = j // 3, pl.ds(pl.multiple_of(lax.rem(j, 3) * 16, 16), 16)
        block = div[rows, pl.ds(pl.multiple_of(xp * 16, 16), 16), :].reshape(256, NY)
        turned = dot(perm[...], block).astype(BF).reshape(16, 16, NY)
        for b in range(16):
            cols = slice(b % 2 * 128, b % 2 * 128 + 128)
            for yh in range(2):
                sbuf[xp * 16 + b // 2 * 2 + yh, rows, cols] = turned[b, :, yh * 128 : yh * 128 + 128]

    pltpu.make_async_copy(div_in, div, lsem.at[0]).wait()
    loop(0, 6, gather_nodes)
    pl.semaphore_wait(barrier, 70)

    own_planes = slab.at[pl.ds(pl.multiple_of(s * 48, 48), 48), :]

    def send1(k):
        dst = span_peer(k)
        remote(sbuf.at[dst], own_planes, ssem1, rsem1, (dst, t))

    pltpu.make_async_copy(sbuf.at[s], own_planes, rsem1).start()
    loop(0, 16, send1)

    pltpu.make_async_copy(flow_in, flow, lsem.at[1]).wait()
    own_rows = gath.at[pl.ds(pl.multiple_of(t * 32, 32), 32), :]
    pltpu.make_async_copy(flow, own_rows, gsem.at[0]).start()
    remote(flow, own_rows, gssem, gsem.at[1], (lax.rem(s + 16, 32), (1 - zh) * 8 + u))
    loop(1, 8, lambda k: remote(flow, own_rows, gssem, gsem.at[0], group_peer(k)))
    loop(17, 32, send1)

    for j, (src, dst) in enumerate(small):
        pltpu.make_async_copy(src, dst, lsem.at[2 + j]).wait()

    def make_table(j):
        i, part = j // 4, j % 4
        rows = pl.ds(pl.multiple_of(j * 128, 128), 128)

        def store(a, values):
            tbl[rows, a * 128 : (a + 1) * 128] = values

        table_rows(i, part, store)

    loop(0, 12, make_table)

    w = wall[...]
    thi[...], tlo[...] = split(w.T)
    wm = jnp.broadcast_to(wmass[...], (128, NY)).T
    fe = jnp.broadcast_to(feig[...], (128, NX)).T
    for j in range(NY // 128):
        cols = slice(j * 128, (j + 1) * 128)
        whi[:, cols], wlo[:, cols] = split(w[:, cols] * wm)
        denom[:, cols] = fe + weig[:, cols]

    far = (1 - zh) * 8 + u
    far_rows = gath.at[pl.ds(pl.multiple_of(far * 32, 32), 32), :]
    wait(far_rows, gsem.at[1])
    loop(1, 8, lambda k: remote(far_rows, far_rows, gssem, gsem.at[2], group_peer(k)))
    wait(gath.at[pl.ds(0, 256), :], gsem.at[0])
    wait(gath.at[pl.ds(0, 224), :], gsem.at[2])

    fhi[...], flo[...] = split(gath[...])
    fm = jnp.broadcast_to(fmass[...], (128, NX)).T
    node = lax.broadcasted_iota(jnp.int32, (NX, NX), 0)
    spot = lax.broadcasted_iota(jnp.int32, (NX, NX), 1)
    came = (node & 257) + ((node >> 5) & 7) * 2 + ((node >> 1) & 15) * 16
    order = jnp.where(came == spot, 1.0, 0.0).astype(BF)
    for j in range(NX // 128):
        cols = slice(j * 128, (j + 1) * 128)
        hi, lo = split((gath[:, cols] * fm).T)
        fmthi[cols, :] = dot(hi, order).astype(BF)
        fmtlo[cols, :] = dot(lo, order).astype(BF)

    def transform(i):
        for part in range(2):
            rows = pl.ds(pl.multiple_of(i * 512 + part * 256, 256), 256)
            r = dot(tbl[rows, :], slab[...]) * F32(float(NZ) ** -0.5)
            spec[pl.ds(part * 4, 4), i] = r.astype(BF).reshape(4, 64, 256)

    def senda(i):
        def one(k):
            uu = lax.rem(u + k, 8)
            remote(spec.at[uu, i], abuf.at[u, i], ssema, rsema.at[i], group_peer(k))

        pltpu.make_async_copy(spec.at[u, i], abuf.at[u, i], rsema.at[i]).start()
        loop(1, 8, one)

    def turn(i):
        wait(abuf.at[:, i], rsema.at[i])
        for q in range(4):
            rows = pl.ds(q * 16, 16)
            tiles = [abuf[b // 2, i, rows, b % 2 * 128 : b % 2 * 128 + 128] for b in range(16)]
            r = dot(perm[...], jnp.concatenate(tiles, axis=0))
            bbuf[i, rows] = r.astype(BF).reshape(16, 16, 128)

    def sendb(i):
        dst_ref = lines.at[i, s % 2, zh * 16 + s // 2]

        def one(k):
            hh, sp = ring_peer(k)
            remote(bbuf.at[i, hh * 32 + sp], dst_ref, ssemb, rsemb.at[i], (sp, hh * 8 + u))

        loop(0, 60, one)
        pltpu.make_async_copy(bbuf.at[i, zh * 32 + s], dst_ref, rsemb.at[i]).start()
        loop(61, 64, one)

    def solve(i):
        for yh in range(2):
            nodes = lines[i, yh].reshape(NX, 128)
            proj[:, yh * 128 : yh * 128 + 128] = dot(fmthi[...], nodes) + dot(fmtlo[...], nodes)
        f = s * 48 + t * 3 + i
        k = jnp.where(f <= NZ // 2, f, f - NZ // 2).astype(F32) / F32(NZ // 2)
        ahi, alo = split(proj[...])
        coeff = dot(ahi, whi[...]) + (dot(ahi, wlo[...]) + dot(alo, whi[...]))
        shi, slo = split(coeff / (denom[...] + k * k))
        back = dot(fhi[...], shi) + (dot(fhi[...], slo) + dot(flo[...], shi))
        bhi, blo = split(back)
        out[i] = dot(bhi, thi[...]) + (dot(bhi, tlo[...]) + dot(blo, thi[...]))

    wait(slab, rsem1)

    def fields(i):
        transform(i)
        senda(i)

    def share(i):
        turn(i)
        sendb(i)

    def finish(i):
        wait(lines.at[i], rsemb.at[i])
        solve(i)
        pltpu.make_async_copy(out.at[i], out_hbm.at[i], osem).start()

    loop(0, 3, fields)
    loop(0, 3, share)
    loop(0, 3, finish)

    wait(gath.at[pl.ds(0, 480), :], gssem)
    wait(slab.at[pl.ds(0, 31 * 48), :], ssem1)
    wait(spec.at[pl.ds(0, 7)], ssema)
    wait(bbuf.at[:, pl.ds(0, 63)], ssemb)
    pltpu.make_async_copy(out, out_hbm, osem).wait()


def local(divergence, flow_basis, wall_basis, flow_mass, wall_mass, flow_eigen, wall_eigen):
    hbm = pl.BlockSpec(memory_space=pl.ANY)
    dma = pltpu.SemaphoreType.DMA
    return pl.pallas_call(
        poisson_kernel,
        out_shape=jax.ShapeDtypeStruct((3, NX, NY), F32),
        in_specs=[hbm] * 7,
        out_specs=hbm,
        scratch_shapes=[
            pltpu.VMEM((48, 32, NY), BF),
            pltpu.VMEM((32, NX), F32),
            pltpu.VMEM((1, NX), F32),
            pltpu.VMEM((NY, NY), F32),
            pltpu.VMEM((1, NY), F32),
            pltpu.VMEM((1, NX), F32),
            pltpu.VMEM((1, NY), F32),
            pltpu.VMEM((3, NX, NY), F32),
            pltpu.VMEM((NZ, NZ), BF),
            pltpu.VMEM((32, 48, 256), BF),
            pltpu.VMEM((NZ, 256), BF),
            pltpu.VMEM((8, 3, 64, 256), BF),
            pltpu.VMEM((8, 3, 64, 256), BF),
            pltpu.VMEM((3, 64, 16, 128), BF),
            pltpu.VMEM((3, 2, 32, 16, 128), BF),
            pltpu.VMEM((NX, NY), F32),
            pltpu.VMEM((NX, NX), F32),
            pltpu.VMEM((256, 256), BF),
            pltpu.VMEM((NX, NX), BF),
            pltpu.VMEM((NX, NX), BF),
            pltpu.VMEM((NY, NY), BF),
            pltpu.VMEM((NY, NY), BF),
            pltpu.VMEM((NY, NY), BF),
            pltpu.VMEM((NY, NY), BF),
            pltpu.VMEM((NX, NX), BF),
            pltpu.VMEM((NX, NX), BF),
            pltpu.VMEM((NX, NY), F32),
            dma,
            dma((3,)),
            dma((3,)),
            dma,
            dma,
            dma,
            dma((3,)),
            dma,
            dma((7,)),
            dma,
        ],
        compiler_params=pltpu.CompilerParams(collective_id=0, has_side_effects=True, vmem_limit_bytes=VMEM_LIMIT),
    )(
        divergence, flow_basis, flow_mass.reshape(1, NX), wall_basis, wall_mass.reshape(1, NY),
        flow_eigen.reshape(1, NX), wall_eigen.reshape(1, NY),
    )


def solution(mesh):
    return jax.shard_map(
        local,
        mesh=mesh,
        in_specs=(P("span", "stream", None), P("stream", None), P(), P(), P(), P(), P()),
        out_specs=P(("span", "stream"), None, None),
        check_vma=False,
    )
```

time: 349 us -> 105 us (0.30)
  waiting for transfers between devices: 147 us -> 0 us
  Pallas kernels: 0 us -> 103 us
  blocking collectives: 82.2 us -> 0 us
  matrix products: 64.8 us -> 0 us
  starting transfers between devices: 28.8 us -> 0 us
  between operations: 13.5 us -> 0.01 us
  local copies, waits for them, and re-layouts: 11.8 us -> 2.65 us
    pallas_call x0 -> x1, Pallas kernels: none -> 103 us  [local(): pl.pallas_call(poisson_kernel, out_shape=jax.ShapeDtypeStruct((3, NX, NY)...]
    all_to_all x2 -> x0, waiting for transfers between devices: 93.8 us -> none  [the longest x1 56 us: local(): lax.all_to_all(grouped, 'stream', split_axis=0, concat_axis=1, tiled=True)]
    all_to_all x1 -> x0, blocking collectives: 82.2 us -> none  [local(): lax.all_to_all(spectral, 'span', split_axis=0, concat_axis=1, tiled=True)]
    dot_general x5 -> x0, matrix products: 64.8 us -> none  [the longest x1 52.7 us: local(): jnp.dot(table, slab_in.reshape(field_count, -1), preferred_element_type=j...]
    all_gather x1 -> x0, waiting for transfers between devices: 52.6 us -> none  [local(): lax.all_gather(flow_basis, 'stream', axis=0, tiled=True)]
    all_to_all x2 -> x0, starting transfers between devices: 28.6 us -> none  [the longest x1 15.9 us: local(): lax.all_to_all(divergence, 'span', split_axis=1, concat_axis=0, tiled=True)]
    reshape x1 -> x0, local copies, waits for them, and re-layouts: 6.46 us -> none  [local(): (flat * float(field_count) ** (-0.5)).reshape(field_count, slab_in.shape[...]
  transfers between devices with their start and end apart: 3 -> 0, of which waited for: 3 -> 0; matrix products, arithmetic and copies ran while one was open for 1% -> 0% of each run, Pallas kernels for 0% -> 0%
where the time goes in v2:
time: 105 us
  Pallas kernels  103 us (98%)
  local copies, waits for them, and re-layouts  2.65 us (3%)
    pallas_call x1, Pallas kernels, local(): pl.pallas_call(poisson_kernel, out_shape=jax.ShapeDtypeStruct((3, NX, NY)...  103 us
    unnamed x1, local copies, waits for them, and re-layouts  2.65 us

profile of v2, /device:TPU:1, one launch (start us, length us, event | category | flops | bytes accessed | tf_op | source)
XLA Modules:
  0.0 105.3 jit_solution(12505430266249045164)
XLA Ops:
  0.0 102.7 %shard_map.73 = f32[3,512,256]{2,1,0:T(8,128)} custom-call(bf16[48,32,256]{2,1,0:T(8,128)(2,1)} %div_in.1, f32[32,512]{1,0:T(8,128)} %flow_in.1, f32[1,512]{1,0:T(1,128)} %bitcast.4, f32[256,256]{1,0:T(8,128)} %wall_in.1, f32[1,256]{1,0:T(1,128)} %bitcast.6, f32[1,512]{1,0:T(1,128)} %bitcast.5, f32[1,256]{1,0:T(1,128)} %bitcast.7), custom_call_target="tpu_custom_call" | custom-call | tf_op jit(solution)/shard_map/pallas_call | solution.py:262
  102.7 2.7 %copy.9 = f32[3,512,256]{2,1,0:T(8,128)} copy(f32[3,512,256]{2,1,0:T(8,128)} %shard_map.73) | data formatting | bytes 3145728

commit v3 on v2

--- a/solution.py
+++ b/solution.py
@@ -29,7 +29,8 @@
 def table_rows(i, part, store):
     row = lax.broadcasted_iota(jnp.int32, (128, 128), 0) + 128 * part
     plane = lax.broadcasted_iota(jnp.int32, (128, 128), 1)
-    field = 48 * (row & 31) + 24 * ((row >> 5) & 1) + 3 * (row >> 6) + i
+    owner = 4 * (row & 7) + 2 * ((row >> 4) & 1) + (row >> 8)
+    field = 48 * owner + 24 * ((row >> 3) & 1) + 3 * ((row >> 5) & 7) + i
     sine = field > NZ // 2
     wavenum = jnp.where(sine, field - NZ // 2, field)
     shift = jnp.where(sine, 1, 0)
@@ -63,7 +64,7 @@
     rsem1, rsema, rsemb, ssem1, ssema, ssemb, gsem, gssem, lsem, osem,
 ):
     s, t = lax.axis_index("span"), lax.axis_index("stream")
-    zl, x = s // 4, s % 4
+    zl, xhi, xlo = s // 4, (s // 2) % 2, s % 2
     zh, u = t // 8, t % 8
     z = zh * 8 + zl
 
@@ -82,13 +83,17 @@
         return lax.rem(s // 16 + 1 + k // 16, 2) * 16 + lax.rem(s + k, 16)
 
     def ring_peer(k):
-        step = k // 4
+        step = k // 2
         hops = jnp.where(step % 2 == 0, 8 - step // 2, 9 + step // 2)
         zz = lax.rem(z + hops, 16)
-        return zz // 8, lax.rem(zz, 8) * 4 + lax.rem(x + k, 4)
+        return zz // 8, lax.rem(zz, 8), lax.rem(xhi + k, 2)
 
     def group_peer(k):
         return s, zh * 8 + lax.rem(u + k, 8)
+
+    def pair_peer(k):
+        place = lax.rem(xlo * 8 + u + k, 16)
+        return place, (s - xlo + place // 8, zh * 8 + lax.rem(place, 8))
 
     pltpu.make_async_copy(div_in, div, lsem.at[0]).start()
     pltpu.make_async_copy(flow_in, flow, lsem.at[1]).start()
@@ -101,13 +106,11 @@
     def greet(peer):
         pl.semaphore_signal(barrier, inc=1, device_id=peer, device_id_type=MESH)
 
-    def greet_ring(k):
-        hh, sp = ring_peer(k)
-        greet((sp, hh * 8 + u))
-
-    loop(0, 60, greet_ring)
-    loop(61, 64, greet_ring)
-    loop(1, 8, lambda k: greet(group_peer(k)))
+    loop(0, 16, lambda k: greet((span_peer(k), t)))
+    loop(17, 32, lambda k: greet((span_peer(k), t)))
+    loop(0, 16, lambda k: greet((2 * k + xlo, (1 - zh) * 8 + u)))
+    loop(0, 7, lambda k: greet((s, zh * 8 + lax.rem(u + 1 + k, 8))))
+    loop(0, 7, lambda k: greet((s + 1 - 2 * xlo, zh * 8 + lax.rem(u + 1 + k, 8))))
 
     i0 = lax.broadcasted_iota(jnp.int32, (256, 256), 0)
     i1 = lax.broadcasted_iota(jnp.int32, (256, 256), 1)
@@ -117,30 +120,34 @@
         xp, rows = j // 3, pl.ds(pl.multiple_of(lax.rem(j, 3) * 16, 16), 16)
         block = div[rows, pl.ds(pl.multiple_of(xp * 16, 16), 16), :].reshape(256, NY)
         turned = dot(perm[...], block).astype(BF).reshape(16, 16, NY)
-        for b in range(16):
-            cols = slice(b % 2 * 128, b % 2 * 128 + 128)
-            for yh in range(2):
-                sbuf[xp * 16 + b // 2 * 2 + yh, rows, cols] = turned[b, :, yh * 128 : yh * 128 + 128]
+        for c in range(2):
+            sbuf[pl.ds(xp * 16, 16), c, rows, :] = turned[:, :, c * 128 : c * 128 + 128]
 
     pltpu.make_async_copy(div_in, div, lsem.at[0]).wait()
     loop(0, 6, gather_nodes)
-    pl.semaphore_wait(barrier, 70)
-
-    own_planes = slab.at[pl.ds(pl.multiple_of(s * 48, 48), 48), :]
-
-    def send1(k):
-        dst = span_peer(k)
-        remote(sbuf.at[dst], own_planes, ssem1, rsem1, (dst, t))
-
-    pltpu.make_async_copy(sbuf.at[s], own_planes, rsem1).start()
-    loop(0, 16, send1)
+    pl.semaphore_wait(barrier, 61)
+
+    own_planes = pl.ds(pl.multiple_of(s * 48, 48), 48)
+
+    def send1(c, first, last):
+        def one(k):
+            dst = span_peer(k)
+            remote(sbuf.at[dst, c], slab.at[c, own_planes], ssem1, rsem1.at[c], (dst, t))
+
+        loop(first, last, one)
+
+    for c in range(2):
+        pltpu.make_async_copy(sbuf.at[s, c], slab.at[c, own_planes], rsem1.at[c]).start()
+    send1(0, 0, 16)
+    send1(0, 17, 32)
 
     pltpu.make_async_copy(flow_in, flow, lsem.at[1]).wait()
     own_rows = gath.at[pl.ds(pl.multiple_of(t * 32, 32), 32), :]
     pltpu.make_async_copy(flow, own_rows, gsem.at[0]).start()
     remote(flow, own_rows, gssem, gsem.at[1], (lax.rem(s + 16, 32), (1 - zh) * 8 + u))
     loop(1, 8, lambda k: remote(flow, own_rows, gssem, gsem.at[0], group_peer(k)))
-    loop(17, 32, send1)
+    send1(1, 0, 16)
+    send1(1, 17, 32)
 
     for j, (src, dst) in enumerate(small):
         pltpu.make_async_copy(src, dst, lsem.at[2 + j]).wait()
@@ -176,7 +183,7 @@
     fm = jnp.broadcast_to(fmass[...], (128, NX)).T
     node = lax.broadcasted_iota(jnp.int32, (NX, NX), 0)
     spot = lax.broadcasted_iota(jnp.int32, (NX, NX), 1)
-    came = (node & 257) + ((node >> 5) & 7) * 2 + ((node >> 1) & 15) * 16
+    came = (node & 256) + ((node >> 1) & 15) * 16 + (node & 1) * 8 + ((node >> 5) & 7)
     order = jnp.where(came == spot, 1.0, 0.0).astype(BF)
     for j in range(NX // 128):
         cols = slice(j * 128, (j + 1) * 128)
@@ -184,75 +191,86 @@
         fmthi[cols, :] = dot(hi, order).astype(BF)
         fmtlo[cols, :] = dot(lo, order).astype(BF)
 
-    def transform(i):
+    def transform(c, i):
         for part in range(2):
             rows = pl.ds(pl.multiple_of(i * 512 + part * 256, 256), 256)
-            r = dot(tbl[rows, :], slab[...]) * F32(float(NZ) ** -0.5)
-            spec[pl.ds(part * 4, 4), i] = r.astype(BF).reshape(4, 64, 256)
-
-    def senda(i):
+            r = dot(tbl[rows, :], slab[c]) * F32(float(NZ) ** -0.5)
+            spec[c, pl.ds(part * 8, 8), i] = r.astype(BF).reshape(8, 32, 128)
+
+    def senda(c, i):
+        here = xlo * 8 + u
+
         def one(k):
-            uu = lax.rem(u + k, 8)
-            remote(spec.at[uu, i], abuf.at[u, i], ssema, rsema.at[i], group_peer(k))
-
-        pltpu.make_async_copy(spec.at[u, i], abuf.at[u, i], rsema.at[i]).start()
-        loop(1, 8, one)
-
-    def turn(i):
-        wait(abuf.at[:, i], rsema.at[i])
-        for q in range(4):
+            place, peer = pair_peer(k)
+            remote(spec.at[c, place, i], abuf.at[c, here, i], ssema, rsema.at[c, i], peer)
+
+        pltpu.make_async_copy(spec.at[c, here, i], abuf.at[c, here, i], rsema.at[c, i]).start()
+        loop(1, 16, one)
+
+    def turn(c, i):
+        wait(abuf.at[c, :, i], rsema.at[c, i])
+        for q in range(2):
             rows = pl.ds(q * 16, 16)
-            tiles = [abuf[b // 2, i, rows, b % 2 * 128 : b % 2 * 128 + 128] for b in range(16)]
-            r = dot(perm[...], jnp.concatenate(tiles, axis=0))
-            bbuf[i, rows] = r.astype(BF).reshape(16, 16, 128)
-
-    def sendb(i):
-        dst_ref = lines.at[i, s % 2, zh * 16 + s // 2]
+            r = dot(perm[...], abuf[c, :, i, rows, :].reshape(256, 128))
+            bbuf[c, i, rows] = r.astype(BF).reshape(16, 16, 128)
+
+    def sendb(c, i):
+        dst_ref = lines.at[c, i, z * 2 + xhi]
 
         def one(k):
-            hh, sp = ring_peer(k)
-            remote(bbuf.at[i, hh * 32 + sp], dst_ref, ssemb, rsemb.at[i], (sp, hh * 8 + u))
-
-        loop(0, 60, one)
-        pltpu.make_async_copy(bbuf.at[i, zh * 32 + s], dst_ref, rsemb.at[i]).start()
-        loop(61, 64, one)
-
-    def solve(i):
-        for yh in range(2):
-            nodes = lines[i, yh].reshape(NX, 128)
-            proj[:, yh * 128 : yh * 128 + 128] = dot(fmthi[...], nodes) + dot(fmtlo[...], nodes)
+            hh, zz, xx = ring_peer(k)
+            remote(
+                bbuf.at[c, i, xx * 16 + hh * 8 + zz], dst_ref, ssemb, rsemb.at[c, i],
+                (zz * 4 + xx * 2 + xlo, hh * 8 + u),
+            )
+
+        loop(0, 30, one)
+        pltpu.make_async_copy(bbuf.at[c, i, xhi * 16 + z], dst_ref, rsemb.at[c, i]).start()
+        one(31)
+
+    def project(c, i):
+        wait(lines.at[c, i], rsemb.at[c, i])
+        nodes = lines[c, i].reshape(NX, 128)
+        hi, lo = split(dot(fmthi[...], nodes) + dot(fmtlo[...], nodes))
+        half = pl.ds(c * 128, 128)
+        return dot(hi, whi[half, :]) + (dot(hi, wlo[half, :]) + dot(lo, whi[half, :]))
+
+    def solve(i, coeff):
         f = s * 48 + t * 3 + i
         k = jnp.where(f <= NZ // 2, f, f - NZ // 2).astype(F32) / F32(NZ // 2)
-        ahi, alo = split(proj[...])
-        coeff = dot(ahi, whi[...]) + (dot(ahi, wlo[...]) + dot(alo, whi[...]))
         shi, slo = split(coeff / (denom[...] + k * k))
         back = dot(fhi[...], shi) + (dot(fhi[...], slo) + dot(flo[...], shi))
         bhi, blo = split(back)
         out[i] = dot(bhi, thi[...]) + (dot(bhi, tlo[...]) + dot(blo, thi[...]))
 
-    wait(slab, rsem1)
-
-    def fields(i):
-        transform(i)
-        senda(i)
-
-    def share(i):
-        turn(i)
-        sendb(i)
+    for c in range(2):
+        wait(slab.at[c], rsem1.at[c])
+
+        def fields(i):
+            transform(c, i)
+            senda(c, i)
+
+        def share(i):
+            turn(c, i)
+            sendb(c, i)
+
+        loop(0, 3, fields)
+        loop(0, 3, share)
+
+    def begin(i):
+        proj[i] = project(0, i)
 
     def finish(i):
-        wait(lines.at[i], rsemb.at[i])
-        solve(i)
+        solve(i, proj[i] + project(1, i))
         pltpu.make_async_copy(out.at[i], out_hbm.at[i], osem).start()
 
-    loop(0, 3, fields)
-    loop(0, 3, share)
+    loop(0, 3, begin)
     loop(0, 3, finish)
 
     wait(gath.at[pl.ds(0, 480), :], gssem)
-    wait(slab.at[pl.ds(0, 31 * 48), :], ssem1)
-    wait(spec.at[pl.ds(0, 7)], ssema)
-    wait(bbuf.at[:, pl.ds(0, 63)], ssemb)
+    wait(slab.at[:, pl.ds(0, 31 * 48), :], ssem1)
+    wait(spec.at[:, pl.ds(0, 15)], ssema)
+    wait(bbuf.at[:, :, pl.ds(0, 31)], ssemb)
     pltpu.make_async_copy(out, out_hbm, osem).wait()
 
 
@@ -274,13 +292,13 @@
             pltpu.VMEM((1, NY), F32),
             pltpu.VMEM((3, NX, NY), F32),
             pltpu.VMEM((NZ, NZ), BF),
-            pltpu.VMEM((32, 48, 256), BF),
-            pltpu.VMEM((NZ, 256), BF),
-            pltpu.VMEM((8, 3, 64, 256), BF),
-            pltpu.VMEM((8, 3, 64, 256), BF),
-            pltpu.VMEM((3, 64, 16, 128), BF),
-            pltpu.VMEM((3, 2, 32, 16, 128), BF),
-            pltpu.VMEM((NX, NY), F32),
+            pltpu.VMEM((32, 2, 48, 128), BF),
+            pltpu.VMEM((2, NZ, 128), BF),
+            pltpu.VMEM((2, 16, 3, 32, 128), BF),
+            pltpu.VMEM((2, 16, 3, 32, 128), BF),
+            pltpu.VMEM((2, 3, 32, 16, 128), BF),
+            pltpu.VMEM((2, 3, 32, 16, 128), BF),
+            pltpu.VMEM((3, NX, NY), F32),
             pltpu.VMEM((NX, NX), F32),
             pltpu.VMEM((256, 256), BF),
             pltpu.VMEM((NX, NX), BF),
@@ -292,9 +310,9 @@
             pltpu.VMEM((NX, NX), BF),
             pltpu.VMEM((NX, NX), BF),
             pltpu.VMEM((NX, NY), F32),
-            dma,
-            dma((3,)),
-            dma((3,)),
+            dma((2,)),
+            dma((2, 3)),
+            dma((2, 3)),
             dma,
             dma,
             dma,

time: 105 us -> 96.6 us (0.920)
  Pallas kernels: 103 us -> 93.8 us
    pallas_call x1, Pallas kernels: 103 us -> 93.8 us  [local(): pl.pallas_call(poisson_kernel, out_shape=jax.ShapeDtypeStruct((3, NX, NY)...]
where the time goes in v3:
time: 96.6 us; the launch traced here: 96.5 us
  Pallas kernels  93.8 us (97%)
  local copies, waits for them, and re-layouts  2.65 us (3%)
    pallas_call x1, Pallas kernels, local(): pl.pallas_call(poisson_kernel, out_shape=jax.ShapeDtypeStruct((3, NX, NY)...  93.8 us
    unnamed x1, local copies, waits for them, and re-layouts  2.65 us

profile of v3, /device:TPU:1, one launch (start us, length us, event | category | flops | bytes accessed | tf_op | source)
XLA Modules:
  0.0 96.5 jit_solution(6779543819098199669)
XLA Ops:
  0.0 93.8 %shard_map.73 = f32[3,512,256]{2,1,0:T(8,128)} custom-call(bf16[48,32,256]{2,1,0:T(8,128)(2,1)} %div_in.1, f32[32,512]{1,0:T(8,128)} %flow_in.1, f32[1,512]{1,0:T(1,128)} %bitcast.4, f32[256,256]{1,0:T(8,128)} %wall_in.1, f32[1,256]{1,0:T(1,128)} %bitcast.6, f32[1,512]{1,0:T(1,128)} %bitcast.5, f32[1,256]{1,0:T(1,128)} %bitcast.7), custom_call_target="tpu_custom_call" | custom-call | tf_op jit(solution)/shard_map/pallas_call | solution.py:280
  93.9 2.7 %copy.9 = f32[3,512,256]{2,1,0:T(8,128)} copy(f32[3,512,256]{2,1,0:T(8,128)} %shard_map.73) | data formatting | bytes 3145728

commit v4 on v3

--- a/solution.py
+++ b/solution.py
@@ -9,7 +9,7 @@
 
 NZ, NX, NY = 1536, 512, 256
 MESH = pl.DeviceIdType.MESH
-VMEM_LIMIT = 63 << 20
+VMEM_LIMIT = 48 << 20
 BF, F32 = jnp.bfloat16, jnp.float32
 
 
@@ -58,10 +58,10 @@
 
 def poisson_kernel(
     div_in, flow_in, fmass_in, wall_in, wmass_in, feig_in, weig_in,
-    out_hbm,
-    div, flow, fmass, wall, wmass, feig, weig, out, tbl, sbuf, slab, spec, abuf, bbuf, lines, proj, gath, perm,
+    out,
+    div, flow, fmass, wall, wmass, feig, weig, tbl, sbuf, slab, spec, abuf, bbuf, lines, proj, gath, perm,
     fhi, flo, whi, wlo, thi, tlo, fmthi, fmtlo, denom,
-    rsem1, rsema, rsemb, ssem1, ssema, ssemb, gsem, gssem, lsem, osem,
+    rsem1, rsema, rsemb, ssem1, ssema, ssemb, gsem, gssem, lsem,
 ):
     s, t = lax.axis_index("span"), lax.axis_index("stream")
     zl, xhi, xlo = s // 4, (s // 2) % 2, s % 2
@@ -262,7 +262,6 @@
 
     def finish(i):
         solve(i, proj[i] + project(1, i))
-        pltpu.make_async_copy(out.at[i], out_hbm.at[i], osem).start()
 
     loop(0, 3, begin)
     loop(0, 3, finish)
@@ -271,17 +270,20 @@
     wait(slab.at[:, pl.ds(0, 31 * 48), :], ssem1)
     wait(spec.at[:, pl.ds(0, 15)], ssema)
     wait(bbuf.at[:, :, pl.ds(0, 31)], ssemb)
-    pltpu.make_async_copy(out, out_hbm, osem).wait()
 
 
 def local(divergence, flow_basis, wall_basis, flow_mass, wall_mass, flow_eigen, wall_eigen):
     hbm = pl.BlockSpec(memory_space=pl.ANY)
     dma = pltpu.SemaphoreType.DMA
+    args = [
+        divergence, flow_basis, flow_mass.reshape(1, NX), wall_basis, wall_mass.reshape(1, NY),
+        flow_eigen.reshape(1, NX), wall_eigen.reshape(1, NY),
+    ]
     return pl.pallas_call(
         poisson_kernel,
         out_shape=jax.ShapeDtypeStruct((3, NX, NY), F32),
         in_specs=[hbm] * 7,
-        out_specs=hbm,
+        out_specs=pl.BlockSpec(memory_space=pltpu.VMEM),
         scratch_shapes=[
             pltpu.VMEM((48, 32, NY), BF),
             pltpu.VMEM((32, NX), F32),
@@ -290,7 +292,6 @@
             pltpu.VMEM((1, NY), F32),
             pltpu.VMEM((1, NX), F32),
             pltpu.VMEM((1, NY), F32),
-            pltpu.VMEM((3, NX, NY), F32),
             pltpu.VMEM((NZ, NZ), BF),
             pltpu.VMEM((32, 2, 48, 128), BF),
             pltpu.VMEM((2, NZ, 128), BF),
@@ -319,13 +320,9 @@
             dma((3,)),
             dma,
             dma((7,)),
-            dma,
         ],
         compiler_params=pltpu.CompilerParams(collective_id=0, has_side_effects=True, vmem_limit_bytes=VMEM_LIMIT),
-    )(
-        divergence, flow_basis, flow_mass.reshape(1, NX), wall_basis, wall_mass.reshape(1, NY),
-        flow_eigen.reshape(1, NX), wall_eigen.reshape(1, NY),
-    )
+    )(*[pltpu.with_memory_space_constraint(a, pltpu.HBM) for a in args])
 
 
 def solution(mesh):

time: 96.6 us -> 94.3 us (0.976)
  local copies, waits for them, and re-layouts: 2.65 us -> 1.15 us
    unnamed x1, local copies, waits for them, and re-layouts: 2.65 us -> 1.15 us
where the time goes in v4:
time: 94.3 us; the launch traced here: 94.2 us
  Pallas kernels  93 us (99%)
  local copies, waits for them, and re-layouts  1.15 us (1%)
    pallas_call x1, Pallas kernels, local(): pl.pallas_call(poisson_kernel, out_shape=jax.ShapeDtypeStruct((3, NX, NY)...  93 us

profile of v4, /device:TPU:1, one launch (start us, length us, event | category | flops | bytes accessed | tf_op | source)
XLA Modules:
  0.0 94.2 jit_solution(14146938392388697305)
XLA Ops:
  0.0 93.0 %shard_map.73 = f32[3,512,256]{2,1,0:T(8,128)S(1)} custom-call(bf16[48,32,256]{2,1,0:T(8,128)(2,1)} %div_in.1, f32[32,512]{1,0:T(8,128)} %flow_in.1, f32[1,512]{1,0:T(1,128)} %bitcast.4, f32[256,256]{1,0:T(8,128)} %wall_in.1, f32[1,256]{1,0:T(1,128)} %bitcast.6, f32[1,512]{1,0:T(1,128)} %bitcast.5, f32[1,256]{1,0:T(1,128)} %bitcast.7), custom_call_target="tpu_custom_call" | custom-call | tf_op jit(solution)/shard_map/pallas_call | solution.py:282
  93.0 1.1 %copy.9 = f32[3,512,256]{2,1,0:T(8,128)} copy(f32[3,512,256]{2,1,0:T(8,128)S(1)} %shard_map.73) | data formatting | bytes 3145728

commit v5 on v4

--- a/solution.py
+++ b/solution.py
@@ -83,7 +83,7 @@
         return lax.rem(s // 16 + 1 + k // 16, 2) * 16 + lax.rem(s + k, 16)
 
     def ring_peer(k):
-        step = k // 2
+        step = 15 - k // 2
         hops = jnp.where(step % 2 == 0, 8 - step // 2, 9 + step // 2)
         zz = lax.rem(z + hops, 16)
         return zz // 8, lax.rem(zz, 8), lax.rem(xhi + k, 2)
@@ -96,11 +96,6 @@
         return place, (s - xlo + place // 8, zh * 8 + lax.rem(place, 8))
 
     pltpu.make_async_copy(div_in, div, lsem.at[0]).start()
-    pltpu.make_async_copy(flow_in, flow, lsem.at[1]).start()
-    small = [(fmass_in, fmass), (wall_in, wall), (wmass_in, wmass), (feig_in, feig), (weig_in, weig)]
-    for j, (src, dst) in enumerate(small):
-        pltpu.make_async_copy(src, dst, lsem.at[2 + j]).start()
-
     barrier = pltpu.get_barrier_semaphore()
 
     def greet(peer):
@@ -112,19 +107,22 @@
     loop(0, 7, lambda k: greet((s, zh * 8 + lax.rem(u + 1 + k, 8))))
     loop(0, 7, lambda k: greet((s + 1 - 2 * xlo, zh * 8 + lax.rem(u + 1 + k, 8))))
 
+    pltpu.make_async_copy(flow_in, flow, lsem.at[1]).start()
+    small = [(fmass_in, fmass), (wall_in, wall), (wmass_in, wmass), (feig_in, feig), (weig_in, weig)]
+    for j, (src, dst) in enumerate(small):
+        pltpu.make_async_copy(src, dst, lsem.at[2 + j]).start()
+
     i0 = lax.broadcasted_iota(jnp.int32, (256, 256), 0)
     i1 = lax.broadcasted_iota(jnp.int32, (256, 256), 1)
     perm[...] = jnp.where(lax.rem(i0, 16) * 16 + i0 // 16 == i1, 1.0, 0.0).astype(BF)
 
-    def gather_nodes(j):
+    def gather_nodes(c, j):
         xp, rows = j // 3, pl.ds(pl.multiple_of(lax.rem(j, 3) * 16, 16), 16)
-        block = div[rows, pl.ds(pl.multiple_of(xp * 16, 16), 16), :].reshape(256, NY)
-        turned = dot(perm[...], block).astype(BF).reshape(16, 16, NY)
-        for c in range(2):
-            sbuf[pl.ds(xp * 16, 16), c, rows, :] = turned[:, :, c * 128 : c * 128 + 128]
+        block = div[rows, pl.ds(pl.multiple_of(xp * 16, 16), 16), c * 128 : c * 128 + 128].reshape(256, 128)
+        sbuf[pl.ds(xp * 16, 16), c, rows, :] = dot(perm[...], block).astype(BF).reshape(16, 16, 128)
 
     pltpu.make_async_copy(div_in, div, lsem.at[0]).wait()
-    loop(0, 6, gather_nodes)
+    loop(0, 6, lambda j: gather_nodes(0, j))
     pl.semaphore_wait(barrier, 61)
 
     own_planes = pl.ds(pl.multiple_of(s * 48, 48), 48)
@@ -136,10 +134,14 @@
 
         loop(first, last, one)
 
-    for c in range(2):
+    def keep(c):
         pltpu.make_async_copy(sbuf.at[s, c], slab.at[c, own_planes], rsem1.at[c]).start()
+
     send1(0, 0, 16)
     send1(0, 17, 32)
+    keep(0)
+    loop(0, 6, lambda j: gather_nodes(1, j))
+    keep(1)
 
     pltpu.make_async_copy(flow_in, flow, lsem.at[1]).wait()
     own_rows = gath.at[pl.ds(pl.multiple_of(t * 32, 32), 32), :]
@@ -224,9 +226,9 @@
                 (zz * 4 + xx * 2 + xlo, hh * 8 + u),
             )
 
-        loop(0, 30, one)
+        one(1)
+        loop(2, 32, one)
         pltpu.make_async_copy(bbuf.at[c, i, xhi * 16 + z], dst_ref, rsemb.at[c, i]).start()
-        one(31)
 
     def project(c, i):
         wait(lines.at[c, i], rsemb.at[c, i])

time: 94.3 us -> 94.3 us (level)
  no operation moved by 1% of the time
where the time goes in v5:
time: 94.3 us; the launch traced here: 94.2 us
  Pallas kernels  93 us (99%)
  local copies, waits for them, and re-layouts  1.15 us (1%)
    pallas_call x1, Pallas kernels, local(): pl.pallas_call(poisson_kernel, out_shape=jax.ShapeDtypeStruct((3, NX, NY)...  93 us

profile of v5, /device:TPU:1, one launch (start us, length us, event | category | flops | bytes accessed | tf_op | source)
XLA Modules:
  0.0 94.2 jit_solution(2626452963499202409)
XLA Ops:
  0.0 93.0 %shard_map.73 = f32[3,512,256]{2,1,0:T(8,128)S(1)} custom-call(bf16[48,32,256]{2,1,0:T(8,128)(2,1)} %div_in.1, f32[32,512]{1,0:T(8,128)} %flow_in.1, f32[1,512]{1,0:T(1,128)} %bitcast.4, f32[256,256]{1,0:T(8,128)} %wall_in.1, f32[1,256]{1,0:T(1,128)} %bitcast.6, f32[1,512]{1,0:T(1,128)} %bitcast.5, f32[1,256]{1,0:T(1,128)} %bitcast.7), custom_call_target="tpu_custom_call" | custom-call | tf_op jit(solution)/shard_map/pallas_call | solution.py:284
  93.0 1.1 %copy.9 = f32[3,512,256]{2,1,0:T(8,128)} copy(f32[3,512,256]{2,1,0:T(8,128)S(1)} %shard_map.73) | data formatting | bytes 3145728
